TPU v7x, 128 devices: a whole 4x4x4 slice. The times are simulated.
128 devices in a mesh: seq: 32 (over x, y, core), head: 4 (over z).
Axes of the slice: x: 4, y: 4, z: 4, core: 2. Of those that a mesh axis runs over, the one named last changes fastest.
Arguments:
- queries: bfloat16 [49152, 4096], P('seq', 'head'), may hold values from -4 to 4
- keys: bfloat16 [49152, 4096], P('seq', 'head'), may hold values from -4 to 4
- values: bfloat16 [49152, 4096], P('seq', 'head'), may hold values from -90 to 90, as said below
- out_grad: bfloat16 [49152, 4096], P('seq', 'head'), may hold values from -4 to 4
Outputs:
- result: bfloat16 [49152, 4096], P('seq', 'head')
- q_grad: bfloat16 [49152, 4096], P('seq', 'head')
- k_grad: bfloat16 [49152, 4096], P('seq', 'head')
- v_grad: bfloat16 [49152, 4096], P('seq', 'head')
Inputs may be any that keep to these rules, and one draw needn't show every extreme that they name: Real values of varying scale over tokens and features.
All inputs are finite; a program needn't handle non-finite values.
Results may differ from a plain program's by a relative error of at most 0.006.
Values sent between devices are 32-bit elements; how exact they have to be, the bound alone decides.
A program may use at most 192 MiB of HBM per device.

v0:
```python
import jax
import jax.numpy as jnp
from jax import lax
from jax.sharding import PartitionSpec as P

NH = 32
HD = 128
GROUP = 128


epsilon = 1e-05


def prefix(value, axis, join, neutral, backward):
    count, mine = (lax.axis_size(axis), lax.axis_index(axis))
    pieces = lax.all_gather(value, axis)
    if backward:
        pieces = pieces[::-1]
        mine = count - 1 - mine
    total = jnp.full_like(value, 0) + jnp.asarray(neutral, value.dtype)

    def lap(position, total):
        longer = join(total, pieces[position])
        return jnp.where(position < mine, longer, total)

    return lax.fori_loop(0, count - 1, lap, total)


def add_states(first_part, second_part):
    return first_part + second_part


def on_device(queries, keys, values, out_grad):
    tok_rows, widths = queries.shape
    local_heads = widths // HD
    group_count = tok_rows // GROUP
    factor = HD ** (-0.5)
    width_all = NH * HD
    shape_four = (group_count, GROUP, local_heads, HD)
    q_blocks = queries.reshape(shape_four)
    k_blocks = keys.reshape(shape_four)
    v_blocks = values.reshape(shape_four)
    causal = lax.broadcasted_iota(jnp.int32, (GROUP, GROUP), 0) >= lax.broadcasted_iota(
        jnp.int32, (GROUP, GROUP), 1
    )
    scores = (
        jnp.einsum("nihd,njhd->nhij", q_blocks, k_blocks, preferred_element_type=jnp.float32)
        * factor
    )
    weights = jnp.where(causal, scores, 0.0).astype(jnp.bfloat16)
    group_states = jnp.einsum(
        "nihd,nihe->nhde", k_blocks, v_blocks, preferred_element_type=jnp.float32
    )
    own_total = jnp.sum(group_states, axis=0)
    inner_prefix = jnp.cumsum(group_states, axis=0) - group_states
    carried = prefix(own_total, "seq", add_states, jnp.zeros_like(own_total), False)
    prefix_bf = (carried[None] + inner_prefix).astype(jnp.bfloat16)
    out_blocks = jnp.einsum(
        "nhij,njhe->nihe", weights, v_blocks, preferred_element_type=jnp.float32
    )
    out_blocks = out_blocks + factor * jnp.einsum(
        "nihd,nhde->nihe", q_blocks, prefix_bf, preferred_element_type=jnp.float32
    )
    out_flat = out_blocks.reshape(tok_rows, widths)
    grad_f = out_grad.astype(jnp.float32)
    local_squares = jnp.sum(out_flat * out_flat, axis=1)
    local_inner = jnp.sum(grad_f * out_flat, axis=1)
    total_squares = lax.psum(local_squares, "head")
    total_inner = lax.psum(local_inner, "head")
    recip = lax.rsqrt(total_squares / width_all + epsilon)
    result = (out_flat * recip[:, None]).astype(jnp.bfloat16)
    grad_raw = recip[:, None] * grad_f - (recip**3 * total_inner / width_all)[:, None] * out_flat
    grad_blocks = grad_raw.astype(jnp.bfloat16).reshape(shape_four)
    dscore = (
        jnp.einsum("nihe,njhe->nhij", grad_blocks, v_blocks, preferred_element_type=jnp.float32)
        * factor
    )
    dscore = jnp.where(causal, dscore, 0.0).astype(jnp.bfloat16)
    q_grad = jnp.einsum("nhij,njhd->nihd", dscore, k_blocks, preferred_element_type=jnp.float32)
    q_grad = q_grad + factor * jnp.einsum(
        "nihe,nhde->nihd", grad_blocks, prefix_bf, preferred_element_type=jnp.float32
    )
    group_grads = factor * jnp.einsum(
        "nihd,nihe->nhde", q_blocks, grad_blocks, preferred_element_type=jnp.float32
    )
    own_grad = jnp.sum(group_grads, axis=0)
    inner_suffix = own_grad[None] - jnp.cumsum(group_grads, axis=0)
    carried_back = prefix(own_grad, "seq", add_states, jnp.zeros_like(own_grad), True)
    suffix_bf = (carried_back[None] + inner_suffix).astype(jnp.bfloat16)
    k_grad = jnp.einsum("nhij,nihd->njhd", dscore, q_blocks, preferred_element_type=jnp.float32)
    k_grad = k_grad + jnp.einsum(
        "nihe,nhde->nihd", v_blocks, suffix_bf, preferred_element_type=jnp.float32
    )
    v_grad = jnp.einsum("nhij,nihe->njhe", weights, grad_blocks, preferred_element_type=jnp.float32)
    v_grad = v_grad + jnp.einsum(
        "nihd,nhde->nihe", k_blocks, suffix_bf, preferred_element_type=jnp.float32
    )
    flat = (tok_rows, widths)
    return (
        result,
        q_grad.reshape(flat).astype(jnp.bfloat16),
        k_grad.reshape(flat).astype(jnp.bfloat16),
        v_grad.reshape(flat).astype(jnp.bfloat16),
    )


def solution(mesh):
    return jax.shard_map(
        on_device,
        mesh=mesh,
        in_specs=(P("seq", "head"), P("seq", "head"), P("seq", "head"), P("seq", "head")),
        out_specs=(P("seq", "head"), P("seq", "head"), P("seq", "head"), P("seq", "head")),
        check_vma=False,
    )
```

profile of v0, /device:TPU:1, one launch (start us, length us, event | category | flops | bytes accessed | tf_op | source)
XLA Modules:
  0.0 353.1 jit_solution(6175431083155911552)
XLA Ops:
  11.0 4.8 %fusion.34 = (f32[8,128,128]{2,1,0:T(8,128)}, f32[12,8,128,128]{3,2,1,0:T(8,128)}) fusion(bf16[12,128,8,128]{3,2,1,0:T(8,128)(2,1)S(1)} %bitcast.94, bf16[12,128,8,128]{3,2,1,0:T(8,128)(2,1)S(1)} %bitcast.90), kind=kOutput, calls=%fused_computation.54 | convolution fusion | flops 404094976 | bytes 13107200 | tf_op jit(solution)/shard_map/nihd,nihe->nhde/dot_general | solution.py:51
  22.9 5.0 %fusion.14 = f32[12,8,128,128]{2,3,1,0:T(8,128)} fusion(bf16[12,8,128,128]{3,2,1,0:T(8,128)(2,1)S(1)} %select_convert_fusion.1, bf16[12,128,8,128]{3,2,1,0:T(8,128)(2,1)S(1)} %bitcast.96), kind=kOutput, calls=%fused_computation.31 | convolution fusion | flops 402653184 | bytes 12582912 | tf_op jit(solution)/shard_map/nhij,njhe->nihe/dot_general | solution.py:58
  27.8 64.2 %all-gather.5.cloned.1.call-done = f32[256,128,128]{2,1,0:T(8,128)} async-done(((f32[8,128,128]{2,1,0:T(8,128)}), f32[256,128,128]{2,1,0:T(8,128)}) %all-gather.5.cloned.1.call-update) | async-done | bytes 16777232 | tf_op jit(solution)/shard_map/all_gather | solution.py:16
  92.0 38.8 %while.28 = (s32[]{:T(128)}, f32[8,128,128]{2,1,0:T(8,128)S(1)}, s32[]{:T(128)}, f32[32,8,128,128]{3,2,1,0:T(8,128)}, s32[]{:T(128)}, /*index=5*/s32[]{:T(128)}) while((s32[]{:T(128)}, f32[8,128,128]{2,1,0:T(8,128)S(1)}, s32[]{:T(128)}, f32[32,8,128,128]{3,2,1,0:T(8,128)}, s32[]{:T(128)}, /*index=5*/s32[]{:T(128)}) %tuple.81), condition=%wide.region_2.3_spmd.clone, body=%wide.region_1.2_spmd.clone.sunk | while | flops 393220 | bytes 1572957 | solution.py:26
  131.6 8.1 %add_convert_fusion.2 = bf16[12,8,128,128]{3,2,1,0:T(8,128)(2,1)} fusion(f32[12,8,128,128]{3,2,1,0:T(8,128)} %get-tuple-element.217, f32[8,128,128]{2,1,0:T(8,128)} %copy-done.15), kind=kOutput, calls=%fused_computation.22 | output fusion | flops 22020096 | bytes 9961472 | tf_op jit(solution)/shard_map/jit(cumsum)/reduce_window_sum | solution.py:55
  139.7 8.5 %multiply_reduce_fusion = (f32[12,128]{1,0:T(8,128)S(1)}, f32[12,128,8,128]{1,3,2,0:T(8,128)}) fusion(bf16[12,8,128,128]{3,2,1,0:T(8,128)(2,1)} %add_convert_fusion.2, bf16[12,128,8,128]{3,2,1,0:T(8,128)(2,1)S(1)} %bitcast.100, f32[12,8,128,128]{2,3,1,0:T(8,128)} %fusion.14), kind=kOutput, calls=%fused_computation.21 | convolution fusion | flops 408943104 | bytes 18880512 | tf_op jit(solution)/shard_map/nihd,nhde->nihe/dot_general | solution.py:61
  148.2 6.7 %copy.92 = f32[12,128,8,128]{3,2,1,0:T(8,128)} copy(f32[12,128,8,128]{1,3,2,0:T(8,128)} %get-tuple-element.219) | data formatting | bytes 12582912 | tf_op jit(solution)/shard_map/add | solution.py:61
  154.9 3.8 %fusion.2 = f32[1536]{0:T(1024)S(1)} fusion(bf16[1536,1024]{1,0:T(8,128)(2,1)S(1)} %copy-done.16, f32[192,8,8,128]{3,2,1,0:T(8,128)} %bitcast.86), kind=kLoop, calls=%fused_computation.6 | loop fusion | flops 4717056 | bytes 9443328 | tf_op jit(solution)/shard_map/reduce_sum | solution.py:67
  158.7 13.4 %all-reduce = (f32[1536]{0:T(1024)S(1)}, f32[1536]{0:T(1024)S(1)}) all-reduce(f32[1536]{0:T(1024)S(1)} %bitcast.112, f32[1536]{0:T(1024)S(1)} %fusion.2), channel_id=1, replica_groups=mesh['seq'=32,'head'=4] {'head'}, use_global_device_ids=true, to_apply=%region_5.6 | all-reduce | flops 3072 | bytes 24576 | tf_op jit(solution)/shard_map/psum | solution.py:68
  172.1 6.2 %fusion.12 = (bf16[192,8,8,128]{3,1,2,0:T(8,128)(2,1)S(1)}, bf16[1536,1024]{1,0:T(8,128)(2,1)}) fusion(f32[192,8,8,128]{3,2,1,0:T(8,128)} %bitcast.87, bf16[1536,1024]{1,0:T(8,128)(2,1)S(1)} %copy-done.16, f32[1536]{0:T(1024)S(1)} %get-tuple-element.214, f32[1536]{0:T(1024)S(1)} %get-tuple-element.215), kind=kLoop, calls=%fused_computation.26 | loop fusion | flops 11010048 | bytes 15740928
  180.8 3.8 %copy.101 = bf16[12,128,8,128]{1,3,2,0:T(8,128)(2,1)S(1)} copy(bf16[12,128,8,128]{3,2,1,0:T(8,128)(2,1)} %bitcast.103) | data formatting | bytes 6291456 | tf_op jit(solution)/shard_map/reshape | solution.py:73
  184.6 6.5 %bitcast_reduce_fusion = (f32[8,128,128]{1,2,0:T(8,128)}, f32[12,8,128,128]{3,2,1,0:T(8,128)}) fusion(bf16[12,128,8,128]{1,3,2,0:T(8,128)(2,1)S(1)} %copy.101, bf16[12,128,8,128]{3,2,1,0:T(8,128)(2,1)} %bitcast.99), kind=kOutput, calls=%fused_computation.14 | convolution fusion | flops 405667840 | bytes 13107200 | tf_op jit(solution)/shard_map/nihd,nihe->nhde/dot_general | solution.py:83
  193.1 4.3 %select_convert_fusion = bf16[12,8,128,128]{3,2,1,0:T(8,128)(2,1)S(1)} fusion(pred[128,128]{1,0:T(8,128)(4,1)S(1)} %iota_compare_fusion, bf16[12,128,8,128]{1,3,2,0:T(8,128)(2,1)S(1)} %copy.101, bf16[12,128,8,128]{3,2,1,0:T(8,128)(2,1)} %bitcast.95), kind=kOutput, calls=%fused_computation.20 | convolution fusion | flops 407371776 | bytes 9453568 | tf_op jit(solution)/shard_map/nihe,njhe->nhij/dot_general | solution.py:75
  203.5 4.9 %copy.98 = bf16[12,128,8,128]{3,2,1,0:T(8,128)(2,1)} copy(bf16[12,128,8,128]{1,3,2,0:T(8,128)(2,1)} %fusion.7) | data formatting | bytes 6291456 | tf_op jit(solution)/shard_map/convert_element_type | solution.py:101
  208.5 4.6 %copy.165 = bf16[192,8,8,128]{3,1,2,0:T(8,128)(2,1)} copy(bf16[192,8,8,128]{3,2,1,0:T(8,128)(2,1)} %bitcast.104) | data formatting | bytes 6291456
  213.1 3.8 %fusion.27 = f32[12,8,128,128]{3,2,1,0:T(8,128)} fusion(bf16[12,8,128,128]{3,2,1,0:T(8,128)(2,1)S(1)} %copy-done.18, bf16[12,128,8,128]{3,2,1,0:T(8,128)(2,1)S(1)} %bitcast.101), kind=kOutput, calls=%fused_computation.44 | convolution fusion | flops 402653184 | bytes 12582912 | tf_op jit(solution)/shard_map/nhij,nihd->njhd/dot_general | solution.py:90
  220.4 46.2 %all-gather.7.cloned.1.call-done = f32[256,128,128]{2,1,0:T(8,128)} async-done(((f32[8,128,128]{2,1,0:T(8,128)}), f32[256,128,128]{2,1,0:T(8,128)}) %all-gather.7.cloned.1.call-update) | async-done | bytes 16777232 | tf_op jit(solution)/shard_map/all_gather | solution.py:16
  266.6 11.7 %rev.3 = f32[32,8,128,128]{3,2,1,0:T(8,128)} reverse(f32[32,8,128,128]{3,2,1,0:T(8,128)} %bitcast.102), dimensions={0} | reverse | bytes 33554432 | tf_op jit(solution)/shard_map/rev | solution.py:18
  278.3 38.8 %while.29 = (s32[]{:T(128)}, f32[8,128,128]{2,1,0:T(8,128)S(1)}, s32[]{:T(128)}, f32[32,8,128,128]{3,2,1,0:T(8,128)}, s32[]{:T(128)}, /*index=5*/s32[]{:T(128)}) while((s32[]{:T(128)}, f32[8,128,128]{2,1,0:T(8,128)S(1)}, s32[]{:T(128)}, f32[32,8,128,128]{3,2,1,0:T(8,128)}, s32[]{:T(128)}, /*index=5*/s32[]{:T(128)}) %tuple.79), condition=%wide.region_10.11_spmd.clone, body=%wide.region_9.10_spmd.clone.sunk | while | flops 393220 | bytes 1572957 | solution.py:26
  317.4 5.7 %add_convert_fusion.1 = bf16[12,8,128,128]{2,3,1,0:T(8,128)(2,1)} fusion(f32[12,8,128,128]{3,2,1,0:T(8,128)} %get-tuple-element.221, f32[8,128,128]{1,2,0:T(8,128)S(1)} %copy-done.19, f32[8,128,128]{1,2,0:T(8,128)S(1)} %copy.104), kind=kOutput, calls=%fused_computation.19 | output fusion | flops 23592960 | bytes 10485760 | tf_op jit(solution)/shard_map/jit(cumsum)/reduce_window_sum | solution.py:87
  323.2 4.9 %fusion.4 = bf16[12,128,8,128]{3,1,2,0:T(8,128)(2,1)S(1)} fusion(f32[12,8,128,128]{3,2,1,0:T(8,128)} %fusion.27, bf16[12,8,128,128]{2,3,1,0:T(8,128)(2,1)} %add_convert_fusion.1, bf16[12,128,8,128]{3,2,1,0:T(8,128)(2,1)S(1)} %bitcast.97), kind=kOutput, calls=%fused_computation.11 | convolution fusion | flops 405798912 | bytes 15728640 | tf_op jit(solution)/shard_map/nihe,nhde->nihd/dot_general | solution.py:91
  330.8 4.0 %fusion.11 = bf16[12,128,8,128]{1,3,2,0:T(8,128)(2,1)} fusion(f32[12,8,128,128]{3,2,1,0:T(8,128)S(1)} %bitcast.89, bf16[12,8,128,128]{2,3,1,0:T(8,128)(2,1)S(1)} %copy-done.9, bf16[12,128,8,128]{3,2,1,0:T(8,128)(2,1)S(1)} %bitcast.93), kind=kOutput, calls=%fused_computation.25 | convolution fusion | flops 405798912 | bytes 15728640 | tf_op jit(solution)/shard_map/nihd,nhde->nihe/dot_general | solution.py:95
  334.8 4.8 %copy.111 = bf16[12,128,8,128]{3,2,1,0:T(8,128)(2,1)} copy(bf16[12,128,8,128]{1,3,2,0:T(8,128)(2,1)} %fusion.11) | data formatting | bytes 6291456 | tf_op jit(solution)/shard_map/convert_element_type | solution.py:103
  339.7 6.7 %copy_bitcast_fusion = (bf16[1536,1024]{1,0:T(8,128)(2,1)}, bf16[1536,1024]{1,0:T(8,128)(2,1)}) fusion(bf16[192,8,8,128]{3,2,1,0:T(8,128)(2,1)} %bitcast.106, bf16[192,8,8,128]{3,2,1,0:T(8,128)(2,1)S(1)} %bitcast.105), kind=kLoop, calls=%fused_computation.27 | loop fusion | bytes 12582912 | tf_op jit(solution)/shard_map/convert_element_type | solution.py:103
  (128 shorter events, 104.8 us)
Async XLA Ops:
  7.2 84.8 %all-gather.5.cloned.1.call-start = ((), (), s32[]{:S(2)}) async-start(), calls=%async_computation | async-start | bytes 17301504 | tf_op jit(solution)/shard_map/all_gather | solution.py:16
  7.2 2.9 copy-start.20
  10.1 8.8 %copy-start = (bf16[192,8,8,128]{3,2,1,0:T(8,128)(2,1)}, bf16[192,8,8,128]{3,2,1,0:T(8,128)(2,1)S(1)}, u32[]{:S(2)}) copy-start(bf16[192,8,8,128]{3,2,1,0:T(8,128)(2,1)S(1)} %copy.118) | copy-start | bytes 9437188
  11.0 4.9 %copy-start.3 = (bf16[192,8,8,128]{3,2,1,0:T(8,128)(2,1)}, bf16[192,8,8,128]{3,2,1,0:T(8,128)(2,1)S(1)}, u32[]{:S(2)}) copy-start(bf16[192,8,8,128]{3,2,1,0:T(8,128)(2,1)S(1)} %copy.119) | copy-start | bytes 9437188
  15.9 250.8 %all-gather.7.cloned.1.call-start = ((), (), s32[]{:S(2)}) async-start(), calls=%async_computation.1 | async-start | bytes 17301504 | tf_op jit(solution)/shard_map/all_gather | solution.py:16
  18.8 2.4 copy-start.6
  18.9 4.0 %copy-start.4 = (bf16[192,8,8,128]{3,2,1,0:T(8,128)(2,1)S(1)}, bf16[192,8,8,128]{3,2,1,0:T(8,128)(2,1)}, u32[]{:S(2)}) copy-start(bf16[192,8,8,128]{3,2,1,0:T(8,128)(2,1)} %copy-done.3) | copy-start | bytes 9437188
  21.2 1.7 copy-start.11
  22.9 69.1 %copy-start.14 = (f32[8,128,128]{2,1,0:T(8,128)S(1)}, f32[8,128,128]{2,1,0:T(8,128)}, u32[]{:S(2)}) copy-start(f32[8,128,128]{2,1,0:T(8,128)} %custom-call) | copy-start | bytes 1572868
  131.6 8.1 %copy-start.7 = (bf16[192,8,8,128]{3,2,1,0:T(8,128)(2,1)S(1)}, bf16[192,8,8,128]{3,2,1,0:T(8,128)(2,1)}, u32[]{:S(2)}) copy-start(bf16[192,8,8,128]{3,2,1,0:T(8,128)(2,1)} %copy-done.6) | copy-start | bytes 9437188
  148.2 6.7 %copy-start.16 = (bf16[1536,1024]{1,0:T(8,128)(2,1)S(1)}, bf16[1536,1024]{1,0:T(8,128)(2,1)}, u32[]{:S(2)}) copy-start(bf16[1536,1024]{1,0:T(8,128)(2,1)} %param.11) | copy-start | bytes 9437188
  193.1 4.4 %copy-start.1 = (bf16[192,8,8,128]{3,2,1,0:T(8,128)(2,1)S(1)}, bf16[192,8,8,128]{3,2,1,0:T(8,128)(2,1)}, u32[]{:S(2)}) copy-start(bf16[192,8,8,128]{3,2,1,0:T(8,128)(2,1)} %copy-done) | copy-start | bytes 9437188
  197.5 2.4 copy-start.17
  197.5 3.0 copy-start.10
  208.5 4.6 %copy-start.8 = (bf16[192,8,8,128]{3,2,1,0:T(8,128)(2,1)S(1)}, bf16[192,8,8,128]{3,2,1,0:T(8,128)(2,1)}, u32[]{:S(2)}) copy-start(bf16[192,8,8,128]{3,2,1,0:T(8,128)(2,1)} %copy-done.6) | copy-start | bytes 9437188
  208.5 4.6 %copy-start.18 = (bf16[12,8,128,128]{3,2,1,0:T(8,128)(2,1)S(1)}, bf16[12,8,128,128]{3,2,1,0:T(8,128)(2,1)}, u32[]{:S(2)}) copy-start(bf16[12,8,128,128]{3,2,1,0:T(8,128)(2,1)} %copy-done.17) | copy-start | bytes 9437188
  213.1 3.8 %copy-start.12 = (bf16[12,8,128,128]{3,2,1,0:T(8,128)(2,1)S(1)}, bf16[12,8,128,128]{3,2,1,0:T(8,128)(2,1)}, u32[]{:S(2)}) copy-start(bf16[12,8,128,128]{3,2,1,0:T(8,128)(2,1)} %copy-done.11) | copy-start | bytes 9437188
  266.6 11.7 %copy-start.13 = (f32[8,128,128]{2,1,0:T(8,128)S(1)}, f32[8,128,128]{2,1,0:T(8,128)}, u32[]{:S(2)}) copy-start(f32[8,128,128]{2,1,0:T(8,128)} %custom-call.1) | copy-start | bytes 1572868
  278.3 39.0 %copy-start.19 = (f32[8,128,128]{1,2,0:T(8,128)S(1)}, f32[8,128,128]{1,2,0:T(8,128)}, u32[]{:S(2)}) copy-start(f32[8,128,128]{1,2,0:T(8,128)} %get-tuple-element.220) | copy-start | bytes 1572868
  317.4 5.8 %copy-start.5 = (bf16[192,8,8,128]{3,2,1,0:T(8,128)(2,1)S(1)}, bf16[192,8,8,128]{3,2,1,0:T(8,128)(2,1)}, u32[]{:S(2)}) copy-start(bf16[192,8,8,128]{3,2,1,0:T(8,128)(2,1)} %copy-done.3) | copy-start | bytes 9437188
  317.4 13.1 %slice-start = ((s8[6291456]{0:T(1024)(128)(4,1)}), s8[2097152]{0:T(1024)(128)(4,1)S(1)}, s32[]{:S(2)}) async-start(s8[6291456]{0:T(1024)(128)(4,1)} %bitcast.88), calls=%async_computation.2 | async-start | bytes 4194304
  323.2 7.4 %slice-start.1 = ((s8[6291456]{0:T(1024)(128)(4,1)}), s8[4194304]{0:T(1024)(128)(4,1)S(1)}, s32[]{:S(2)}) async-start(s8[6291456]{0:T(1024)(128)(4,1)} %bitcast.88), calls=%async_computation.3 | async-start | bytes 8388608
  328.0 2.5 copy-start.2
  328.0 2.8 copy-start.9
  (1 other events, 0.8 us)
Sparse Core Ops, SparseCore 0:
  16.0 75.9 all-gather.4
  193.2 73.3 all-gather.6
where the time goes:
time: 357 us; the launch traced here: 353 us
  waiting for transfers between devices  110 us (31%)
  other arithmetic  100 us (28%)
  local copies, waits for them, and re-layouts  60.3 us (17%)
  matrix products  53 us (15%)
  between operations  14.3 us (4%)
  blocking collectives  13.4 us (4%)
    all_gather x2, waiting for transfers between devices, prefix(): pieces = lax.all_gather(value, axis)  110 us
    select_n x62, other arithmetic, lap(): return jnp.where(position < mine, longer, total)  76.1 us
    unnamed x51, local copies, waits for them, and re-layouts  17 us
    psum x1, blocking collectives, on_device(): total_squares = lax.psum(local_squares, 'head')  13.4 us
    rev x1, local copies, waits for them, and re-layouts, prefix(): pieces = pieces[::-1]  11.7 us
    convert_element_type x2, local copies, waits for them, and re-layouts, on_device(): v_grad.reshape(flat).astype(jnp.bfloat16)  11.5 us
    dot_general x1, matrix products, on_device(): jnp.einsum('nihd,nhde->nihe', q_blocks, prefix_bf, preferred_element_type...  8.48 us
    another operation x1, other arithmetic, on_device(): inner_prefix = jnp.cumsum(group_states, axis=0) - group_states  8.14 us
  transfers between devices with their start and end apart: 2, of which 2 were waited for; matrix products, arithmetic and copies ran while one was open for 10% of the time, Pallas kernels for 0%

commit v1 on v0

v1 whole, which is shorter than its diff:
```python
import functools

import jax
import jax.numpy as jnp
from jax import lax
from jax.experimental import pallas as pl
from jax.experimental.pallas import tpu as pltpu
from jax.sharding import PartitionSpec as P

HD = 128
CHUNK = 256
SUB = 128
STAGES = 2
EPSILON = 1e-05

MESH = pl.DeviceIdType.MESH
F32 = jnp.float32
BF16 = jnp.bfloat16
MIB = 1 << 20


def nn(a, b):
    return lax.dot_general(a, b, (((1,), (0,)), ((), ())), preferred_element_type=F32)


def nt(a, b):
    return lax.dot_general(a, b, (((1,), (1,)), ((), ())), preferred_element_type=F32)


def tn(a, b):
    return lax.dot_general(a, b, (((0,), (0,)), ((), ())), preferred_element_type=F32)


def tile(ref, chunk, head):
    row, col = chunk * CHUNK, head * HD
    if not isinstance(row, int):
        row = pl.multiple_of(row, CHUNK)
    if not isinstance(col, int):
        col = pl.multiple_of(col, HD)
    return ref.at[pl.ds(row, CHUNK), pl.ds(col, HD)]


class Scan:
    def __init__(self, refs, heads, backward):
        self.tot, self.pin, self.mine, self.got, self.pre, self.back, self.snd, self.carry = refs[:8]
        self.pair_s, self.pair_r, self.gat_s, self.gat_r, self.ret_s, self.ret_r, self.fin_s, self.fin_r = refs[8:]
        self.half = heads // 2
        self.width = self.half // STAGES
        self.backward = backward
        self.chips = lax.axis_size("seq") // 2
        seq = lax.axis_index("seq")
        self.core = seq % 2
        self.chip = seq // 2
        self.partner = self.chip * 2 + 1 - self.core
        self.later = (1 - self.core if backward else self.core).astype(F32)

    def own(self, stage):
        return self.core * self.half + stage * self.width

    def other(self, stage):
        return (1 - self.core) * self.half + stage * self.width

    def copy(self, src, dst, send, recv, seq):
        return pltpu.make_async_remote_copy(
            src_ref=src, dst_ref=dst, send_sem=send, recv_sem=recv, device_id={"seq": seq}, device_id_type=MESH
        )

    def pair(self, stage):
        return self.copy(
            self.tot.at[pl.ds(self.other(stage), self.width)],
            self.pin.at[stage],
            self.pair_s.at[stage],
            self.pair_r.at[stage],
            self.partner,
        )

    def gather(self, stage, step):
        chip = (self.chip + step) % self.chips
        return self.copy(
            self.mine.at[stage, chip],
            self.got.at[stage, self.chip],
            self.gat_s.at[stage, step],
            self.gat_r.at[stage, step],
            chip * 2 + self.core,
        )

    def give(self, stage, step):
        chip = (self.chip + step) % self.chips
        return self.copy(
            self.pre.at[stage, chip],
            self.back.at[stage, self.chip],
            self.ret_s.at[stage, step],
            self.ret_r.at[stage, step],
            chip * 2 + self.core,
        )

    def finish(self, stage):
        return self.copy(
            self.snd.at[stage],
            self.carry.at[pl.ds(self.own(stage), self.width)],
            self.fin_s.at[stage],
            self.fin_r.at[stage],
            self.partner,
        )

    def add_pair(self, stage):
        self.pair(stage).wait_recv()
        total = self.tot[pl.ds(self.own(stage), self.width)] + self.pin[stage]
        self.mine[stage] = total.reshape(self.mine.shape[1:])
        for step in range(1, self.chips):
            self.gather(stage, step).start()
        self.got[stage, self.chip] = self.mine[stage, self.chip]

    def add_chips(self, stage):
        for step in range(1, self.chips):
            self.gather(stage, step).wait_recv()
        order = range(self.chips)
        total = jnp.zeros(self.got.shape[2:], F32)
        for chip in reversed(order) if self.backward else order:
            self.pre[stage, chip] = total
            total = total + self.got[stage, chip]
        for step in range(1, self.chips):
            self.give(stage, step).start()
        self.back[stage, self.chip] = self.pre[stage, self.chip]

    def hand_over(self, stage):
        for step in range(1, self.chips):
            self.give(stage, step).wait_recv()
        before = self.back[stage].reshape((self.width, HD, HD))
        own = pl.ds(self.own(stage), self.width)
        self.snd[stage] = before + (1.0 - self.later) * self.tot[own]
        self.finish(stage).start()
        self.carry[own] = before + self.later * self.pin[stage]

    def arrive(self, stage):
        self.finish(stage).wait_recv()

    def drain(self):
        for stage in range(STAGES):
            self.pair(stage).wait_send()
            self.finish(stage).wait_send()
            for step in range(1, self.chips):
                self.gather(stage, step).wait_send()
                self.give(stage, step).wait_send()


def scan_scratch(heads, chips):
    half = heads // 2
    width = half // STAGES
    rows = width * HD // chips
    dma = pltpu.SemaphoreType.DMA
    return [
        pltpu.VMEM((heads, HD, HD), F32),
        pltpu.VMEM((STAGES, width, HD, HD), F32),
        pltpu.VMEM((STAGES, chips, rows, HD), F32),
        pltpu.VMEM((STAGES, chips, rows, HD), F32),
        pltpu.VMEM((STAGES, chips, rows, HD), F32),
        pltpu.VMEM((STAGES, chips, rows, HD), F32),
        pltpu.VMEM((STAGES, width, HD, HD), F32),
        pltpu.VMEM((heads, HD, HD), F32),
        dma((STAGES,)),
        dma((STAGES,)),
        dma((STAGES, chips)),
        dma((STAGES, chips)),
        dma((STAGES, chips)),
        dma((STAGES, chips)),
        dma((STAGES,)),
        dma((STAGES,)),
    ]


SCAN_REFS = 16


def split(x):
    high = x.astype(BF16)
    return high, (x - high.astype(F32)).astype(BF16)


def main_kernel(q_hbm, k_hbm, v_hbm, g_hbm, res, qg, kp, vp, k, v, sfx, *scratch):
    q, g, w, pre, pre_bf, norm, norm_in, in_sem, norm_s, norm_r = scratch[:10]
    fwd_refs = scratch[10 : 10 + SCAN_REFS]
    bwd_refs = scratch[10 + SCAN_REFS :]
    out = vp
    rows, width = q.shape
    heads, chunks = width // HD, rows // CHUNK
    factor = HD ** (-0.5)
    heads_all = heads * lax.axis_size("head")
    zs = lax.axis_size("head")
    z = lax.axis_index("head")
    forward = Scan(fwd_refs, heads, False)
    backward = Scan(bwd_refs, heads, True)
    seq, core, chip, chips = lax.axis_index("seq"), forward.core, forward.chip, forward.chips
    per = forward.width

    order = []
    for stage in range(STAGES):
        order += [forward.other(stage), forward.own(stage)]

    def load(which, part):
        src, dst = ((k_hbm, k), (v_hbm, v), (q_hbm, q), (g_hbm, g))[which]
        cols = pl.ds(pl.multiple_of(order[part] * HD, HD), per * HD)
        return pltpu.make_async_copy(src.at[:, cols], dst.at[:, cols], in_sem.at[which, part])

    for part in range(2 * STAGES):
        load(0, part).start()
        load(1, part).start()
    for part in range(2 * STAGES):
        load(2, part).start()
    for part in range(2 * STAGES):
        load(3, part).start()

    barrier = pltpu.get_barrier_semaphore()
    pl.semaphore_signal(barrier, inc=1, device_id={"seq": forward.partner}, device_id_type=MESH)
    for step in range(1, chips):
        pl.semaphore_signal(
            barrier, inc=1, device_id={"seq": ((chip + step) % chips) * 2 + core}, device_id_type=MESH
        )
    for step in range(1, zs):
        pl.semaphore_signal(barrier, inc=1, device_id={"head": (z + step) % zs}, device_id_type=MESH)

    def states(left, right, scan, first, chunk_order):
        def one(i, _):
            head = first + i
            total = jnp.zeros((HD, HD), F32)
            for c in chunk_order:
                pre[head, c] = total
                total = total + tn(tile(left, c, head)[...], tile(right, c, head)[...])
            scan.tot[head] = total
            return 0

        lax.fori_loop(0, per, one, 0)

    up, down = list(range(chunks)), list(reversed(range(chunks)))

    def kv(part):
        load(0, part).wait()
        load(1, part).wait()
        states(k, v, forward, order[part], up)

    row_at = lax.broadcasted_iota(jnp.int32, (SUB, SUB), 0)
    col_at = lax.broadcasted_iota(jnp.int32, (SUB, SUB), 1)
    causal = row_at >= col_at

    def masked(x):
        lines = []
        blocks = CHUNK // SUB
        for i in range(blocks):
            line = []
            for j in range(blocks):
                block = x[i * SUB : (i + 1) * SUB, j * SUB : (j + 1) * SUB] * factor
                if j > i:
                    line.append(jnp.zeros((SUB, SUB), BF16))
                elif j == i:
                    line.append(jnp.where(causal, block, 0.0).astype(BF16))
                else:
                    line.append(block.astype(BF16))
            lines.append(jnp.concatenate(line, axis=1))
        return jnp.concatenate(lines, axis=0)

    def local_forward(low, high):
        def one(head, _):
            for c in range(chunks):
                weights = masked(nt(tile(q, c, head)[...], tile(k, c, head)[...]))
                w[head, c] = weights
                tile(out, c, head)[...] = nn(weights, tile(v, c, head)[...])
            return 0

        lax.fori_loop(low, high, one, 0)

    kv(0)
    pl.semaphore_wait(barrier, chips - 1 + zs)
    forward.pair(0).start()
    kv(1)
    kv(2)
    forward.pair(1).start()
    forward.add_pair(0)
    kv(3)
    forward.add_pair(1)
    for part in range(2 * STAGES):
        load(2, part).wait()
    local_forward(0, heads // 2)
    forward.add_chips(0)
    forward.add_chips(1)
    for part in range(2 * STAGES):
        load(3, part).wait()
    local_forward(heads // 2, heads - 1)
    forward.hand_over(0)
    forward.hand_over(1)
    local_forward(heads - 1, heads)
    forward.arrive(0)
    forward.arrive(1)

    picks = lax.broadcasted_iota(jnp.int32, (8, 4 * HD), 0) // 4 == lax.broadcasted_iota(
        jnp.int32, (8, 4 * HD), 1
    ) // (2 * HD)
    picks = jnp.where(picks, 1.0, 0.0).astype(BF16)

    def norm_copy(c, step):
        return pltpu.make_async_remote_copy(
            src_ref=norm.at[c],
            dst_ref=norm_in.at[step - 1, c],
            send_sem=norm_s.at[step - 1, c],
            recv_sem=norm_r.at[step - 1, c],
            device_id={"head": (z + step) % zs},
            device_id_type=MESH,
        )

    def outputs(i, _):
        c = chunks - 1 - i
        squares = jnp.zeros((CHUNK, HD), F32)
        inner = jnp.zeros((CHUNK, HD), F32)
        for head in range(heads):
            state = (forward.carry[head] + pre[head, c]).astype(BF16)
            pre_bf[head, c] = state
            at = tile(out, c, head)
            value = at[...] + factor * nn(tile(q, c, head)[...], state)
            at[...] = value
            squares = squares + value * value
            inner = inner + tile(g, c, head)[...].astype(F32) * value
        parts = jnp.concatenate(split(squares) + split(inner), axis=1)
        norm[c] = nt(picks, parts)
        for step in range(1, zs):
            norm_copy(c, step).start()
        return 0

    lax.fori_loop(0, chunks, outputs, 0)

    def grads(i, _):
        c = chunks - 1 - i
        total = norm[c]
        for step in range(1, zs):
            norm_copy(c, step).wait_recv()
            total = total + norm_in[step - 1, c]
        squares, inner = total[0:1], total[4:5]
        recip = lax.rsqrt(squares / (heads_all * HD) + EPSILON)
        coef = recip * recip * recip * inner / (heads_all * HD)
        both = jnp.concatenate(
            [jnp.broadcast_to(recip, (4, CHUNK)), jnp.broadcast_to(coef, (4, CHUNK))], axis=0
        ).T
        recip, coef = both[:, 0:1], both[:, 4:5]
        for head in range(heads):
            value = tile(out, c, head)[...]
            at = tile(g, c, head)
            tile(res, c, head)[...] = (value * recip).astype(BF16)
            at[...] = (recip * at[...].astype(F32) - coef * value).astype(BF16)
        return 0

    lax.fori_loop(0, chunks, grads, 0)

    def local_backward(low, high):
        def one(head, _):
            for c in range(chunks):
                grad = tile(g, c, head)[...]
                keys = tile(k, c, head)[...]
                scores = masked(nt(grad, tile(v, c, head)[...]))
                tile(qg, c, head)[...] = (nn(scores, keys) + factor * nt(grad, pre_bf[head, c])).astype(BF16)
                tile(kp, c, head)[...] = tn(scores, tile(q, c, head)[...])
                tile(vp, c, head)[...] = tn(w[head, c], grad)
            return 0

        lax.fori_loop(low, high, one, 0)

    def qg_states(part):
        states(q, g, backward, order[part], down)

    qg_states(0)
    backward.pair(0).start()
    qg_states(1)
    qg_states(2)
    backward.pair(1).start()
    backward.add_pair(0)
    qg_states(3)
    backward.add_pair(1)
    local_backward(0, 3)
    backward.add_chips(0)
    backward.add_chips(1)
    local_backward(3, 6)
    backward.hand_over(0)
    backward.hand_over(1)
    local_backward(6, heads)
    backward.arrive(0)
    backward.arrive(1)

    def suffixes(head, _):
        for c in range(chunks):
            sfx[head, c] = (factor * (backward.carry[head] + pre[head, c])).astype(BF16)
        return 0

    lax.fori_loop(0, heads, suffixes, 0)

    forward.drain()
    backward.drain()
    for c in range(chunks):
        for step in range(1, zs):
            norm_copy(c, step).wait_send()


def last_kernel(res, qg, kp, vp, k, v, sfx, res_o, qg_o, kg_o, vg_o, kg, vg, sems):
    rows, width = k.shape
    heads, chunks = width // HD, rows // CHUNK
    whole = [pltpu.make_async_copy(res, res_o, sems.at[0, 0]), pltpu.make_async_copy(qg, qg_o, sems.at[1, 0])]
    for copy in whole:
        copy.start()

    def leave(which, c):
        src, dst = ((kg, kg_o), (vg, vg_o))[which]
        at = pl.ds(pl.multiple_of(c * CHUNK, CHUNK), CHUNK)
        return pltpu.make_async_copy(src.at[at], dst.at[at], sems.at[2 + which, c])

    def one(c, _):
        for head in range(heads):
            state = sfx[head, c]
            tile(kg, c, head)[...] = (tile(kp, c, head)[...] + nt(tile(v, c, head)[...], state)).astype(BF16)
            tile(vg, c, head)[...] = (tile(vp, c, head)[...] + nn(tile(k, c, head)[...], state)).astype(BF16)
        leave(0, c).start()
        leave(1, c).start()
        return 0

    lax.fori_loop(0, chunks, one, 0)
    for copy in whole:
        copy.wait()
    for c in range(chunks):
        leave(0, c).wait()
        leave(1, c).wait()


def on_device(queries, keys, values, out_grad):
    rows, width = queries.shape
    heads, chunks = width // HD, rows // CHUNK
    chips, zs = lax.axis_size("seq") // 2, lax.axis_size("head")
    dma = pltpu.SemaphoreType.DMA
    flat, flat32 = pltpu.VMEM((rows, width), BF16), pltpu.VMEM((rows, width), F32)
    in_hbm = pl.BlockSpec(memory_space=pltpu.HBM)
    in_vmem = pl.BlockSpec(memory_space=pltpu.VMEM)
    pair = rows * heads * HD * HD * 2
    held = pl.pallas_call(
        main_kernel,
        out_shape=(flat, flat, flat32, flat32, flat, flat, pltpu.VMEM((heads, chunks, HD, HD), BF16)),
        in_specs=[in_hbm] * 4,
        out_specs=[in_vmem] * 7,
        scratch_shapes=[
            flat,
            flat,
            pltpu.VMEM((heads, chunks, CHUNK, CHUNK), BF16),
            pltpu.VMEM((heads, chunks, HD, HD), F32),
            pltpu.VMEM((heads, chunks, HD, HD), BF16),
            pltpu.VMEM((chunks, 8, CHUNK), F32),
            pltpu.VMEM((zs - 1, chunks, 8, CHUNK), F32),
            dma((4, 2 * STAGES)),
            dma((zs - 1, chunks)),
            dma((zs - 1, chunks)),
        ]
        + scan_scratch(heads, chips)
        + scan_scratch(heads, chips),
        compiler_params=pltpu.CompilerParams(
            collective_id=0, has_side_effects=True, vmem_limit_bytes=26 * MIB
        ),
        cost_estimate=pl.CostEstimate(flops=10 * pair, bytes_accessed=8 * rows * width, transcendentals=0),
        name="attention",
    )(queries, keys, values, out_grad)
    held = [pltpu.with_memory_space_constraint(x, pltpu.VMEM) for x in held]
    like = jax.ShapeDtypeStruct((rows, width), BF16)
    return pl.pallas_call(
        last_kernel,
        out_shape=(like,) * 4,
        in_specs=[in_vmem] * 7,
        out_specs=[in_hbm] * 4,
        scratch_shapes=[flat, flat, dma((4, chunks))],
        compiler_params=pltpu.CompilerParams(vmem_limit_bytes=12 * MIB),
        cost_estimate=pl.CostEstimate(flops=2 * pair, bytes_accessed=8 * rows * width, transcendentals=0),
        name="suffix_gradients",
    )(*held)


def solution(mesh):
    spec = P("seq", "head")
    return jax.shard_map(on_device, mesh=mesh, in_specs=(spec,) * 4, out_specs=(spec,) * 4, check_vma=False)
```

time: 357 us -> 59 us (0.17); the launches traced: 353 us -> 58.9 us
  waiting for transfers between devices: 110 us -> 0 us
  other arithmetic: 100 us -> 0 us
  local copies, waits for them, and re-layouts: 60.3 us -> 0 us
  Pallas kernels: 0 us -> 58.2 us
  matrix products: 53 us -> 0 us
  between operations: 14.3 us -> 0.64 us
  blocking collectives: 13.4 us -> 0 us
    all_gather x2 -> x0, waiting for transfers between devices: 110 us -> none  [prefix(): pieces = lax.all_gather(value, axis)]
    select_n x62 -> x0, other arithmetic: 76.1 us -> none  [lap(): return jnp.where(position < mine, longer, total)]
    pallas_call x0 -> x2, Pallas kernels: none -> 58.2 us  [the longest x1 53.4 us: on_device(): pl.pallas_call(main_kernel, out_shape=(flat, flat, flat32, flat32, flat,...]
    dot_general x12 -> x0, matrix products: 53 us -> none  [the longest x1 8.48 us: on_device(): jnp.einsum('nihd,nhde->nihe', q_blocks, prefix_bf, preferred_element_type...]
    convert_element_type x4 -> x0, local copies, waits for them, and re-layouts: 18.8 us -> none  [the longest x2 11.5 us: on_device(): v_grad.reshape(flat).astype(jnp.bfloat16)]
    unnamed x51 -> x0, local copies, waits for them, and re-layouts: 17 us -> none
    another operation x2 -> x0, other arithmetic: 13.9 us -> none  [the longest x1 8.14 us: on_device(): inner_prefix = jnp.cumsum(group_states, axis=0) - group_states]
    psum x1 -> x0, blocking collectives: 13.4 us -> none  [on_device(): total_squares = lax.psum(local_squares, 'head')]
  transfers between devices with their start and end apart: 2 -> 0, of which waited for: 2 -> 0; matrix products, arithmetic and copies ran while one was open for 10% -> 0% of each run, Pallas kernels for 0% -> 0%
where the time goes in v1:
time: 59 us; the launch traced here: 58.9 us
  Pallas kernels  58.2 us (99%)
  between operations  0.64 us (1%)
    pallas_call x1, Pallas kernels, on_device(): pl.pallas_call(main_kernel, out_shape=(flat, flat, flat32, flat32, flat,...  53.4 us
    pallas_call x1, Pallas kernels, on_device(): pl.pallas_call(last_kernel, out_shape=(like,) * 4, in_specs=[in_vmem] * 7...  4.81 us

profile of v1, /device:TPU:1, one launch (start us, length us, event | category | flops | bytes accessed | tf_op | source)
XLA Modules:
  0.0 58.9 jit_solution(11842752101053448831)
XLA Ops:
  0.6 53.4 %attention.1 = (bf16[1536,1024]{1,0:T(8,128)(2,1)S(1)}, bf16[1536,1024]{1,0:T(8,128)(2,1)S(1)}, f32[1536,1024]{1,0:T(8,128)S(1)}, f32[1536,1024]{1,0:T(8,128)S(1...) custom-call(bf16[1536,1024]{1,0:T(8,128)(2,1)} %q_hbm.1, ...), custom_call_target="tpu_custom_call" | custom-call | flops 4026531840 | bytes 12582912 | tf_op jit(solution)/shard_map/attention/pallas_call | solution.py:437
  54.1 4.8 %suffix_gradients.1 = (bf16[1536,1024]{1,0:T(8,128)(2,1)}, bf16[1536,1024]{1,0:T(8,128)(2,1)}, bf16[1536,1024]{1,0:T(8,128)(2,1)}, bf16[1536,1024]{1,0:T(8,128)(2,1)}) custom-call(bf16[1536,1024]{1,0:T(8,128)(2,1)S(1)} %get-tuple-element.11.res, bf16[1536,1024]{1,0:T(8,128)(2,1)S(1)} %get-tuple-element.12.qg, f32[1536,1024]{1,0:T(8,128)S(1)} %get-tuple-element.13.kp, ...), custom_call_target="tpu_custom_call" | custom-call | flops 805306368 | bytes 12582912 | tf_op jit(solution)/shard_map/suffix_gradients/pallas_call | solution.py:464

commit v2 on v1

v2 whole, which is shorter than its diff:
```python
import functools

import jax
import jax.numpy as jnp
from jax import lax
from jax.experimental import pallas as pl
from jax.experimental.pallas import tpu as pltpu
from jax.sharding import PartitionSpec as P

HD = 128
CHUNK = 256
SUB = 128
STAGES = 2
GROUP_HEADS = 4
COLUMNS = 4
NORM_BLOCKS = 4
EPSILON = 1e-05

MESH = pl.DeviceIdType.MESH
F32 = jnp.float32
BF16 = jnp.bfloat16
MIB = 1 << 20


def nn(a, b):
    return lax.dot_general(a, b, (((1,), (0,)), ((), ())), preferred_element_type=F32)


def nt(a, b):
    return lax.dot_general(a, b, (((1,), (1,)), ((), ())), preferred_element_type=F32)


def tn(a, b):
    return lax.dot_general(a, b, (((0,), (0,)), ((), ())), preferred_element_type=F32)


def tile(ref, chunk, head):
    row, col = chunk * CHUNK, head * HD
    if not isinstance(row, int):
        row = pl.multiple_of(row, CHUNK)
    if not isinstance(col, int):
        col = pl.multiple_of(col, HD)
    return ref.at[pl.ds(row, CHUNK), pl.ds(col, HD)]


class Scan:
    def __init__(self, refs, heads, backward):
        self.tot, self.pin, self.mine, self.got, self.pre, self.back, self.snd, self.carry = refs[:8]
        self.pair_s, self.pair_r, self.gat_s, self.gat_r, self.ret_s, self.ret_r, self.fin_s, self.fin_r = refs[8:]
        self.half = heads // 2
        self.width = self.half // STAGES
        self.backward = backward
        self.chips = lax.axis_size("seq") // 2
        self.columns = min(COLUMNS, self.chips // 2)
        self.lines = self.chips // self.columns
        self.offsets = sorted(
            ((i, j) for i in range(self.lines) for j in range(self.columns) if i or j),
            key=lambda at: -(min(at[0], self.lines - at[0]) + min(at[1], self.columns - at[1])),
        )
        seq = lax.axis_index("seq")
        self.core = seq % 2
        self.chip = seq // 2
        self.partner = self.chip * 2 + 1 - self.core
        self.later = (1 - self.core if backward else self.core).astype(F32)

    def own(self, stage):
        return self.core * self.half + stage * self.width

    def other(self, stage):
        return (1 - self.core) * self.half + stage * self.width

    def copy(self, src, dst, send, recv, seq):
        return pltpu.make_async_remote_copy(
            src_ref=src, dst_ref=dst, send_sem=send, recv_sem=recv, device_id={"seq": seq}, device_id_type=MESH
        )

    def pair(self, stage):
        return self.copy(
            self.tot.at[pl.ds(self.other(stage), self.width)],
            self.pin.at[stage],
            self.pair_s.at[stage],
            self.pair_r.at[stage],
            self.partner,
        )

    def chip_at(self, offset):
        x = (self.chip // self.columns + offset[0]) % self.lines
        return x * self.columns + (self.chip + offset[1]) % self.columns

    def gather(self, stage, offset):
        chip = self.chip_at(offset)
        return self.copy(
            self.mine.at[stage, chip],
            self.got.at[stage, self.chip],
            self.gat_s.at[stage],
            self.gat_r.at[stage],
            chip * 2 + self.core,
        )

    def give(self, stage, offset):
        chip = self.chip_at(offset)
        return self.copy(
            self.pre.at[stage, chip],
            self.back.at[stage, self.chip],
            self.ret_s.at[stage],
            self.ret_r.at[stage],
            chip * 2 + self.core,
        )

    def all_gathered(self, stage):
        at = pl.ds(0, self.chips - 1)
        return self.copy(
            self.mine.at[stage, at], self.got.at[stage, at], self.gat_s.at[stage], self.gat_r.at[stage], self.partner
        )

    def all_given(self, stage):
        at = pl.ds(0, self.chips - 1)
        return self.copy(
            self.pre.at[stage, at], self.back.at[stage, at], self.ret_s.at[stage], self.ret_r.at[stage], self.partner
        )

    def finish(self, stage):
        return self.copy(
            self.snd.at[stage],
            self.carry.at[pl.ds(self.own(stage), self.width)],
            self.fin_s.at[stage],
            self.fin_r.at[stage],
            self.partner,
        )

    def add_pair(self, stage):
        self.pair(stage).wait_recv()
        total = self.tot[pl.ds(self.own(stage), self.width)] + self.pin[stage]
        self.mine[stage] = total.reshape(self.mine.shape[1:])
        for offset in self.offsets:
            self.gather(stage, offset).start()
        self.got[stage, self.chip] = self.mine[stage, self.chip]

    def add_chips(self, stage):
        self.all_gathered(stage).wait_recv()
        order = range(self.chips)
        total = jnp.zeros(self.got.shape[2:], F32)
        for chip in reversed(order) if self.backward else order:
            self.pre[stage, chip] = total
            total = total + self.got[stage, chip]
        for offset in self.offsets:
            self.give(stage, offset).start()
        self.back[stage, self.chip] = self.pre[stage, self.chip]

    def hand_over(self, stage):
        self.all_given(stage).wait_recv()
        before = self.back[stage].reshape((self.width, HD, HD))
        own = pl.ds(self.own(stage), self.width)
        self.snd[stage] = before + (1.0 - self.later) * self.tot[own]
        self.finish(stage).start()
        self.carry[own] = before + self.later * self.pin[stage]

    def arrive(self, stage):
        self.finish(stage).wait_recv()

    def drain(self):
        for stage in range(STAGES):
            self.pair(stage).wait_send()
            self.finish(stage).wait_send()
            self.all_gathered(stage).wait_send()
            self.all_given(stage).wait_send()


def scan_scratch(heads, chips):
    half = heads // 2
    width = half // STAGES
    rows = width * HD // chips
    dma = pltpu.SemaphoreType.DMA
    return [
        pltpu.VMEM((heads, HD, HD), F32),
        pltpu.VMEM((STAGES, width, HD, HD), F32),
        pltpu.VMEM((STAGES, chips, rows, HD), F32),
        pltpu.VMEM((STAGES, chips, rows, HD), F32),
        pltpu.VMEM((STAGES, chips, rows, HD), F32),
        pltpu.VMEM((STAGES, chips, rows, HD), F32),
        pltpu.VMEM((STAGES, width, HD, HD), F32),
        pltpu.VMEM((heads, HD, HD), F32),
        dma((STAGES,)),
        dma((STAGES,)),
        dma((STAGES,)),
        dma((STAGES,)),
        dma((STAGES,)),
        dma((STAGES,)),
        dma((STAGES,)),
        dma((STAGES,)),
    ]


SCAN_REFS = 16


def split(x, count):
    terms = []
    for _ in range(count):
        terms.append(x.astype(BF16))
        x = x - terms[-1].astype(F32)
    return terms


def main_kernel(q_hbm, k_hbm, v_hbm, g_hbm, res, qg, kp, vp, k, v, sfx, *scratch):
    q, g, w, pre, pre_bf, recips, coefs, norm, norm_in, in_sem, norm_s, norm_r = scratch[:12]
    fwd_refs = scratch[12 : 12 + SCAN_REFS]
    bwd_refs = scratch[12 + SCAN_REFS :]
    out = vp
    rows, width = q.shape
    heads, chunks = width // HD, rows // CHUNK
    factor = HD ** (-0.5)
    zs = lax.axis_size("head")
    z = lax.axis_index("head")
    features = heads * zs * HD
    forward = Scan(fwd_refs, heads, False)
    backward = Scan(bwd_refs, heads, True)
    core, chips = forward.core, forward.chips
    per = forward.width

    order = []
    for stage in range(STAGES):
        order.append(forward.other(stage))
    for stage in range(STAGES):
        order.append(forward.own(stage))
    parts = len(order)

    def load(which, part):
        src, dst = ((k_hbm, k), (v_hbm, v), (q_hbm, q), (g_hbm, g))[which]
        cols = pl.ds(pl.multiple_of(order[part] * HD, HD), per * HD)
        return pltpu.make_async_copy(src.at[:, cols], dst.at[:, cols], in_sem.at[which, part])

    def load_start(which):
        for part in range(parts):
            load(which, part).start()

    def load_wait(which):
        for part in range(parts):
            load(which, part).wait()

    for part in range(parts):
        load(0, part).start()
        load(1, part).start()
    barrier = pltpu.get_barrier_semaphore()
    pl.semaphore_signal(barrier, inc=1, device_id={"seq": forward.partner}, device_id_type=MESH)
    for offset in forward.offsets:
        pl.semaphore_signal(
            barrier, inc=1, device_id={"seq": forward.chip_at(offset) * 2 + core}, device_id_type=MESH
        )
    for step in range(1, zs):
        pl.semaphore_signal(barrier, inc=1, device_id={"head": (z + step) % zs}, device_id_type=MESH)

    up, down = list(range(chunks)), list(reversed(range(chunks)))

    def kv(part):
        load(0, part).wait()
        load(1, part).wait()
        for i in range(per):
            head = order[part] + i
            total = jnp.zeros((HD, HD), F32)
            for c in up:
                pre[head, c] = total
                total = total + tn(tile(k, c, head)[...], tile(v, c, head)[...])
            forward.tot[head] = total

    row_at = lax.broadcasted_iota(jnp.int32, (SUB, SUB), 0)
    col_at = lax.broadcasted_iota(jnp.int32, (SUB, SUB), 1)
    causal = row_at >= col_at

    def masked(x):
        lines = []
        blocks = CHUNK // SUB
        for i in range(blocks):
            line = []
            for j in range(blocks):
                block = x[i * SUB : (i + 1) * SUB, j * SUB : (j + 1) * SUB] * factor
                if j > i:
                    line.append(jnp.zeros((SUB, SUB), BF16))
                elif j == i:
                    line.append(jnp.where(causal, block, 0.0).astype(BF16))
                else:
                    line.append(block.astype(BF16))
            lines.append(jnp.concatenate(line, axis=1))
        return jnp.concatenate(lines, axis=0)

    def each(body, group=GROUP_HEADS, first=0, last=None):
        def step(i, _):
            for j in range(group):
                for c in range(chunks):
                    body(i * group + j, c)
            return 0

        lax.fori_loop(first // group, (heads if last is None else last) // group, step, 0)

    def flipped(matrix, right):
        lines = []
        for i in range(CHUNK // SUB):
            at = pl.ds(i * SUB, SUB)
            low = pl.ds(i * SUB, CHUNK - i * SUB)
            lines.append(tn(matrix[low, at], right[low, :]))
        return jnp.concatenate(lines, axis=0)

    def scores_step(head, c):
        w[head, c] = masked(nt(tile(q, c, head)[...], tile(k, c, head)[...]))

    def local_step(head, c):
        state = pre[head, c].astype(BF16)
        tile(out, c, head)[...] = nn(w[head, c], tile(v, c, head)[...]) + factor * nn(tile(q, c, head)[...], state)

    kv(0)
    pl.semaphore_wait(barrier, chips - 1 + zs)
    forward.pair(0).start()
    kv(1)
    forward.pair(1).start()
    load_start(2)
    kv(2)
    forward.add_pair(0)
    kv(3)
    forward.add_pair(1)
    load_start(3)
    load_wait(2)
    each(scores_step)
    each(local_step)
    forward.add_chips(0)
    forward.add_chips(1)
    load_wait(3)
    forward.hand_over(0)
    forward.hand_over(1)

    blocks = rows // SUB

    def at_block(b):
        return pl.ds(pl.multiple_of(b * SUB, SUB), SUB)

    def iotas(shape):
        return lax.broadcasted_iota(jnp.int32, shape, 0), lax.broadcasted_iota(jnp.int32, shape, 1)

    def ones_where(condition):
        return jnp.where(condition, 1.0, 0.0).astype(BF16)

    r, c_ = iotas((2 * NORM_BLOCKS, 4 * HD))
    gather_rows = [
        ones_where(r == j + jnp.where(c_ < 2 * HD, 0, NORM_BLOCKS)) for j in range(NORM_BLOCKS)
    ]
    r, c_ = iotas((6 * NORM_BLOCKS, 2 * HD))
    spread_rows = [
        ones_where((r % NORM_BLOCKS == j) & ((r < 3 * NORM_BLOCKS) == (c_ < HD))) for j in range(NORM_BLOCKS)
    ]

    def norm_copy(i, step):
        return pltpu.make_async_remote_copy(
            src_ref=norm.at[i],
            dst_ref=norm_in.at[step - 1, i],
            send_sem=norm_s.at[step - 1, i],
            recv_sem=norm_r.at[step - 1, i],
            device_id={"head": (z + step) % zs},
            device_id_type=MESH,
        )

    def outputs(stage):
        for i in range(2):
            for j in range(per):
                head = order[stage + STAGES * i] + j
                state = forward.carry[head].astype(BF16)
                for c in up:
                    at = tile(out, c, head)
                    at[...] = at[...] + factor * nn(tile(q, c, head)[...], state)

    def row_sums(i, _):
        total = jnp.zeros((2 * NORM_BLOCKS, SUB), F32)
        for j in range(NORM_BLOCKS):
            at = at_block(i * NORM_BLOCKS + j)
            squares, inner = jnp.zeros((SUB, HD), F32), jnp.zeros((SUB, HD), F32)
            for head in range(heads):
                cols = pl.ds(head * HD, HD)
                value = out[at, cols]
                squares = squares + value * value
                inner = inner + g[at, cols].astype(F32) * value
            total = total + nt(gather_rows[j], jnp.concatenate(split(squares, 2) + split(inner, 2), axis=1))
        norm[i] = total
        for to in range(1, zs):
            norm_copy(i, to).start()
        return 0

    for stage in range(STAGES):
        forward.arrive(stage)
        outputs(stage)
    lax.fori_loop(0, blocks // NORM_BLOCKS, row_sums, 0)

    def prefix_step(head, c):
        pre_bf[head, c] = (forward.carry[head] + pre[head, c]).astype(BF16)

    each(prefix_step)

    for i in range(blocks // NORM_BLOCKS):
        total = norm[i]
        for step in range(1, zs):
            norm_copy(i, step).wait_recv()
            total = total + norm_in[step - 1, i]
        squares, inner = total[:NORM_BLOCKS], total[NORM_BLOCKS:]
        recip = lax.rsqrt(squares / features + EPSILON)
        coef = recip * recip * recip * inner / features
        terms = jnp.concatenate([x.astype(F32) for x in split(recip, 3) + split(coef, 3)], axis=0).astype(BF16)
        for j in range(NORM_BLOCKS):
            at = at_block(i * NORM_BLOCKS + j)
            both = tn(terms, spread_rows[j])
            recips[at] = both[:, :HD]
            coefs[at] = both[:, HD:]

    def grad_step(head, c):
        value, recip = tile(out, c, head)[...], recips[pl.ds(c * CHUNK, CHUNK)]
        at = tile(g, c, head)
        at[...] = (recip * at[...].astype(F32) - coefs[pl.ds(c * CHUNK, CHUNK)] * value).astype(BF16)

    def result_step(head, c):
        tile(res, c, head)[...] = (tile(out, c, head)[...] * recips[pl.ds(c * CHUNK, CHUNK)]).astype(BF16)

    def grads(part):
        for i in range(per):
            total = jnp.zeros((HD, HD), F32)
            for c in down:
                if part < parts:
                    grad_step(order[part] + i, c)
                if part > 0:
                    head = order[part - 1] + i
                    pre[head, c] = total
                    total = total + tn(tile(q, c, head)[...], tile(g, c, head)[...])
            if part > 0:
                backward.tot[order[part - 1] + i] = total

    def v_step(head, c):
        tile(vp, c, head)[...] = flipped(w.at[head, c], tile(g, c, head))

    def dscore_step(head, c):
        w[head, c] = masked(nt(tile(g, c, head)[...], tile(v, c, head)[...]))

    def q_step(head, c):
        tile(qg, c, head)[...] = (
            nn(w[head, c], tile(k, c, head)[...]) + factor * nt(tile(g, c, head)[...], pre_bf[head, c])
        ).astype(BF16)

    def k_step(head, c):
        tile(kp, c, head)[...] = flipped(w.at[head, c], tile(q, c, head))

    grads(0)
    grads(1)
    backward.pair(0).start()
    grads(2)
    backward.pair(1).start()
    grads(3)
    backward.add_pair(0)
    grads(4)
    backward.add_pair(1)
    each(result_step)
    each(v_step)
    each(dscore_step)
    each(k_step)
    backward.add_chips(0)
    backward.add_chips(1)
    each(q_step)
    backward.hand_over(0)
    backward.hand_over(1)
    backward.arrive(0)
    backward.arrive(1)

    def suffix_step(head, c):
        sfx[head, c] = (factor * (backward.carry[head] + pre[head, c])).astype(BF16)

    each(suffix_step)

    forward.drain()
    backward.drain()
    for i in range(blocks // NORM_BLOCKS):
        for step in range(1, zs):
            norm_copy(i, step).wait_send()


def last_kernel(res, qg, kp, vp, k, v, sfx, res_o, qg_o, kg_o, vg_o, kg, vg, sems):
    rows, width = k.shape
    heads, chunks = width // HD, rows // CHUNK
    whole = [pltpu.make_async_copy(res, res_o, sems.at[0, 0]), pltpu.make_async_copy(qg, qg_o, sems.at[1, 0])]
    for copy in whole:
        copy.start()

    def leave(which, c):
        src, dst = ((kg, kg_o), (vg, vg_o))[which]
        at = pl.ds(c * CHUNK, CHUNK)
        return pltpu.make_async_copy(src.at[at], dst.at[at], sems.at[2 + which, c])

    for c in range(chunks):
        for head in range(heads):
            state = sfx[head, c]
            tile(kg, c, head)[...] = (tile(kp, c, head)[...] + nt(tile(v, c, head)[...], state)).astype(BF16)
            tile(vg, c, head)[...] = (tile(vp, c, head)[...] + nn(tile(k, c, head)[...], state)).astype(BF16)
        leave(0, c).start()
        leave(1, c).start()
    for copy in whole:
        copy.wait()
    for c in range(chunks):
        leave(0, c).wait()
        leave(1, c).wait()


def on_device(queries, keys, values, out_grad):
    rows, width = queries.shape
    heads, chunks, sums = width // HD, rows // CHUNK, rows // (SUB * NORM_BLOCKS)
    chips, zs = lax.axis_size("seq") // 2, lax.axis_size("head")
    dma = pltpu.SemaphoreType.DMA
    flat, flat32 = pltpu.VMEM((rows, width), BF16), pltpu.VMEM((rows, width), F32)
    in_hbm = pl.BlockSpec(memory_space=pltpu.HBM)
    in_vmem = pl.BlockSpec(memory_space=pltpu.VMEM)
    pair = rows * heads * HD * HD * 2
    held = pl.pallas_call(
        main_kernel,
        out_shape=(flat, flat, flat32, flat32, flat, flat, pltpu.VMEM((heads, chunks, HD, HD), BF16)),
        in_specs=[in_hbm] * 4,
        out_specs=[in_vmem] * 7,
        scratch_shapes=[
            flat,
            flat,
            pltpu.VMEM((heads, chunks, CHUNK, CHUNK), BF16),
            pltpu.VMEM((heads, chunks, HD, HD), F32),
            pltpu.VMEM((heads, chunks, HD, HD), BF16),
            pltpu.VMEM((rows, HD), F32),
            pltpu.VMEM((rows, HD), F32),
            pltpu.VMEM((sums, 2 * NORM_BLOCKS, SUB), F32),
            pltpu.VMEM((zs - 1, sums, 2 * NORM_BLOCKS, SUB), F32),
            dma((4, 2 * STAGES)),
            dma((zs - 1, sums)),
            dma((zs - 1, sums)),
        ]
        + scan_scratch(heads, chips)
        + scan_scratch(heads, chips),
        compiler_params=pltpu.CompilerParams(
            collective_id=0, has_side_effects=True, vmem_limit_bytes=27 * MIB
        ),
        cost_estimate=pl.CostEstimate(flops=10 * pair, bytes_accessed=8 * rows * width, transcendentals=0),
        name="attention",
    )(queries, keys, values, out_grad)
    held = [pltpu.with_memory_space_constraint(x, pltpu.VMEM) for x in held]
    like = jax.ShapeDtypeStruct((rows, width), BF16)
    return pl.pallas_call(
        last_kernel,
        out_shape=(like,) * 4,
        in_specs=[in_vmem] * 7,
        out_specs=[in_hbm] * 4,
        scratch_shapes=[flat, flat, dma((4, chunks))],
        compiler_params=pltpu.CompilerParams(vmem_limit_bytes=12 * MIB),
        cost_estimate=pl.CostEstimate(flops=2 * pair, bytes_accessed=8 * rows * width, transcendentals=0),
        name="suffix_gradients",
    )(*held)


def solution(mesh):
    spec = P("seq", "head")
    return jax.shard_map(on_device, mesh=mesh, in_specs=(spec,) * 4, out_specs=(spec,) * 4, check_vma=False)
```

time: 59 us -> 56.3 us (0.954)
  Pallas kernels: 58.2 us -> 55.3 us
    pallas_call x1, Pallas kernels: 53.4 us -> 50.5 us  [on_device(): pl.pallas_call(main_kernel, out_shape=(flat, flat, flat32, flat32, flat,...]
where the time goes in v2:
time: 56.3 us; the launch traced here: 56.1 us
  Pallas kernels  55.3 us (98%)
  between operations  0.82 us (1%)
    pallas_call x1, Pallas kernels, on_device(): pl.pallas_call(main_kernel, out_shape=(flat, flat, flat32, flat32, flat,...  50.5 us
    pallas_call x1, Pallas kernels, on_device(): pl.pallas_call(last_kernel, out_shape=(like,) * 4, in_specs=[in_vmem] * 7...  4.81 us

profile of v2, /device:TPU:1, one launch (start us, length us, event | category | flops | bytes accessed | tf_op | source)
XLA Modules:
  0.0 56.1 jit_solution(5964141384267088967)
XLA Ops:
  0.6 50.5 %attention.1 = (bf16[1536,1024]{1,0:T(8,128)(2,1)S(1)}, bf16[1536,1024]{1,0:T(8,128)(2,1)S(1)}, f32[1536,1024]{1,0:T(8,128)S(1)}, f32[1536,1024]{1,0:T(8,128)S(1...) custom-call(bf16[1536,1024]{1,0:T(8,128)(2,1)} %q_hbm.1, ...), custom_call_target="tpu_custom_call" | custom-call | flops 4026531840 | bytes 12582912 | tf_op jit(solution)/shard_map/attention/pallas_call | solution.py:513
  51.1 4.8 %suffix_gradients.1 = (bf16[1536,1024]{1,0:T(8,128)(2,1)}, bf16[1536,1024]{1,0:T(8,128)(2,1)}, bf16[1536,1024]{1,0:T(8,128)(2,1)}, bf16[1536,1024]{1,0:T(8,128)(2,1)}) custom-call(bf16[1536,1024]{1,0:T(8,128)(2,1)S(1)} %get-tuple-element.11.res, bf16[1536,1024]{1,0:T(8,128)(2,1)S(1)} %get-tuple-element.12.qg, f32[1536,1024]{1,0:T(8,128)S(1)} %get-tuple-element.13.kp, ...), custom_call_target="tpu_custom_call" | custom-call | flops 805306368 | bytes 12582912 | tf_op jit(solution)/shard_map/suffix_gradients/pallas_call | solution.py:542

commit v3 on v2

--- a/solution.py
+++ b/solution.py
@@ -207,6 +207,8 @@
     fwd_refs = scratch[12 : 12 + SCAN_REFS]
     bwd_refs = scratch[12 + SCAN_REFS :]
     out = vp
+    near = kp
+    given = qg
     rows, width = q.shape
     heads, chunks = width // HD, rows // CHUNK
     factor = HD ** (-0.5)
@@ -226,7 +228,7 @@
     parts = len(order)
 
     def load(which, part):
-        src, dst = ((k_hbm, k), (v_hbm, v), (q_hbm, q), (g_hbm, g))[which]
+        src, dst = ((k_hbm, k), (v_hbm, v), (q_hbm, q), (g_hbm, given))[which]
         cols = pl.ds(pl.multiple_of(order[part] * HD, HD), per * HD)
         return pltpu.make_async_copy(src.at[:, cols], dst.at[:, cols], in_sem.at[which, part])
 
@@ -305,7 +307,7 @@
 
     def local_step(head, c):
         state = pre[head, c].astype(BF16)
-        tile(out, c, head)[...] = nn(w[head, c], tile(v, c, head)[...]) + factor * nn(tile(q, c, head)[...], state)
+        tile(near, c, head)[...] = nn(w[head, c], tile(v, c, head)[...]) + factor * nn(tile(q, c, head)[...], state)
 
     kv(0)
     pl.semaphore_wait(barrier, chips - 1 + zs)
@@ -320,12 +322,11 @@
     load_start(3)
     load_wait(2)
     each(scores_step)
-    each(local_step)
+    each(local_step, last=heads // 2)
     forward.add_chips(0)
     forward.add_chips(1)
+    each(local_step, first=heads // 2)
     load_wait(3)
-    forward.hand_over(0)
-    forward.hand_over(1)
 
     blocks = rows // SUB
 
@@ -357,14 +358,12 @@
             device_id_type=MESH,
         )
 
-    def outputs(stage):
-        for i in range(2):
-            for j in range(per):
-                head = order[stage + STAGES * i] + j
-                state = forward.carry[head].astype(BF16)
-                for c in up:
-                    at = tile(out, c, head)
-                    at[...] = at[...] + factor * nn(tile(q, c, head)[...], state)
+    def outputs(part):
+        for i in range(per):
+            head = order[part] + i
+            state = forward.carry[head].astype(BF16)
+            for c in up:
+                tile(out, c, head)[...] = tile(near, c, head)[...] + factor * nn(tile(q, c, head)[...], state)
 
     def row_sums(i, _):
         total = jnp.zeros((2 * NORM_BLOCKS, SUB), F32)
@@ -375,13 +374,16 @@
                 cols = pl.ds(head * HD, HD)
                 value = out[at, cols]
                 squares = squares + value * value
-                inner = inner + g[at, cols].astype(F32) * value
+                inner = inner + given[at, cols].astype(F32) * value
             total = total + nt(gather_rows[j], jnp.concatenate(split(squares, 2) + split(inner, 2), axis=1))
         norm[i] = total
         for to in range(1, zs):
             norm_copy(i, to).start()
         return 0
 
+    for stage in range(STAGES):
+        forward.hand_over(stage)
+        outputs(STAGES + stage)
     for stage in range(STAGES):
         forward.arrive(stage)
         outputs(stage)
@@ -409,8 +411,8 @@
 
     def grad_step(head, c):
         value, recip = tile(out, c, head)[...], recips[pl.ds(c * CHUNK, CHUNK)]
-        at = tile(g, c, head)
-        at[...] = (recip * at[...].astype(F32) - coefs[pl.ds(c * CHUNK, CHUNK)] * value).astype(BF16)
+        grad = recip * tile(given, c, head)[...].astype(F32) - coefs[pl.ds(c * CHUNK, CHUNK)] * value
+        tile(g, c, head)[...] = grad.astype(BF16)
 
     def result_step(head, c):
         tile(res, c, head)[...] = (tile(out, c, head)[...] * recips[pl.ds(c * CHUNK, CHUNK)]).astype(BF16)
@@ -454,25 +456,29 @@
     each(result_step)
     each(v_step)
     each(dscore_step)
-    each(k_step)
     backward.add_chips(0)
     backward.add_chips(1)
+    each(k_step)
     each(q_step)
-    backward.hand_over(0)
-    backward.hand_over(1)
-    backward.arrive(0)
-    backward.arrive(1)
-
-    def suffix_step(head, c):
-        sfx[head, c] = (factor * (backward.carry[head] + pre[head, c])).astype(BF16)
-
-    each(suffix_step)
-
     forward.drain()
-    backward.drain()
     for i in range(blocks // NORM_BLOCKS):
         for step in range(1, zs):
             norm_copy(i, step).wait_send()
+
+    def suffixes(part):
+        for i in range(per):
+            head = order[part] + i
+            state = backward.carry[head]
+            for c in up:
+                sfx[head, c] = (factor * (state + pre[head, c])).astype(BF16)
+
+    for stage in range(STAGES):
+        backward.hand_over(stage)
+        suffixes(STAGES + stage)
+    for stage in range(STAGES):
+        backward.arrive(stage)
+        suffixes(stage)
+    backward.drain()
 
 
 def last_kernel(res, qg, kp, vp, k, v, sfx, res_o, qg_o, kg_o, vg_o, kg, vg, sems):

time: 56.3 us -> 51.6 us (0.917)
  Pallas kernels: 55.3 us -> 50.6 us
    pallas_call x1, Pallas kernels: 50.5 us -> 45.8 us  [on_device(): pl.pallas_call(main_kernel, out_shape=(flat, flat, flat32, flat32, flat,...]
where the time goes in v3:
time: 51.6 us; the launch traced here: 51.4 us
  Pallas kernels  50.6 us (98%)
  between operations  0.82 us (2%)
    pallas_call x1, Pallas kernels, on_device(): pl.pallas_call(main_kernel, out_shape=(flat, flat, flat32, flat32, flat,...  45.8 us
    pallas_call x1, Pallas kernels, on_device(): pl.pallas_call(last_kernel, out_shape=(like,) * 4, in_specs=[in_vmem] * 7...  4.81 us

profile of v3, /device:TPU:1, one launch (start us, length us, event | category | flops | bytes accessed | tf_op | source)
XLA Modules:
  0.0 51.4 jit_solution(16136345765521268857)
XLA Ops:
  0.6 45.8 %attention.1 = (bf16[1536,1024]{1,0:T(8,128)(2,1)S(1)}, bf16[1536,1024]{1,0:T(8,128)(2,1)S(1)}, f32[1536,1024]{1,0:T(8,128)S(1)}, f32[1536,1024]{1,0:T(8,128)S(1...) custom-call(bf16[1536,1024]{1,0:T(8,128)(2,1)} %q_hbm.1, ...), custom_call_target="tpu_custom_call" | custom-call | flops 4026531840 | bytes 12582912 | tf_op jit(solution)/shard_map/attention/pallas_call | solution.py:519
  46.4 4.8 %suffix_gradients.1 = (bf16[1536,1024]{1,0:T(8,128)(2,1)}, bf16[1536,1024]{1,0:T(8,128)(2,1)}, bf16[1536,1024]{1,0:T(8,128)(2,1)}, bf16[1536,1024]{1,0:T(8,128)(2,1)}) custom-call(bf16[1536,1024]{1,0:T(8,128)(2,1)S(1)} %get-tuple-element.11.res, bf16[1536,1024]{1,0:T(8,128)(2,1)S(1)} %get-tuple-element.12.qg, f32[1536,1024]{1,0:T(8,128)S(1)} %get-tuple-element.13.kp, ...), custom_call_target="tpu_custom_call" | custom-call | flops 805306368 | bytes 12582912 | tf_op jit(solution)/shard_map/suffix_gradients/pallas_call | solution.py:548

commit v4 on v3

--- a/solution.py
+++ b/solution.py
@@ -309,29 +309,28 @@
         state = pre[head, c].astype(BF16)
         tile(near, c, head)[...] = nn(w[head, c], tile(v, c, head)[...]) + factor * nn(tile(q, c, head)[...], state)
 
-    kv(0)
-    pl.semaphore_wait(barrier, chips - 1 + zs)
-    forward.pair(0).start()
-    kv(1)
-    forward.pair(1).start()
+    for stage in range(STAGES):
+        kv(stage)
+        if stage == 0:
+            pl.semaphore_wait(barrier, chips - 1 + zs)
+        forward.pair(stage).start()
     load_start(2)
-    kv(2)
-    forward.add_pair(0)
-    kv(3)
-    forward.add_pair(1)
+    for stage in range(STAGES):
+        kv(STAGES + stage)
+        forward.add_pair(stage)
     load_start(3)
     load_wait(2)
     each(scores_step)
     each(local_step, last=heads // 2)
-    forward.add_chips(0)
-    forward.add_chips(1)
+    for stage in range(STAGES):
+        forward.add_chips(stage)
     each(local_step, first=heads // 2)
     load_wait(3)
 
     blocks = rows // SUB
 
     def at_block(b):
-        return pl.ds(pl.multiple_of(b * SUB, SUB), SUB)
+        return pl.ds(b * SUB, SUB)
 
     def iotas(shape):
         return lax.broadcasted_iota(jnp.int32, shape, 0), lax.broadcasted_iota(jnp.int32, shape, 1)
@@ -365,7 +364,7 @@
             for c in up:
                 tile(out, c, head)[...] = tile(near, c, head)[...] + factor * nn(tile(q, c, head)[...], state)
 
-    def row_sums(i, _):
+    def row_sums(i):
         total = jnp.zeros((2 * NORM_BLOCKS, SUB), F32)
         for j in range(NORM_BLOCKS):
             at = at_block(i * NORM_BLOCKS + j)
@@ -377,9 +376,8 @@
                 inner = inner + given[at, cols].astype(F32) * value
             total = total + nt(gather_rows[j], jnp.concatenate(split(squares, 2) + split(inner, 2), axis=1))
         norm[i] = total
-        for to in range(1, zs):
+        for to in sorted(range(1, zs), key=lambda to: -min(to, zs - to)):
             norm_copy(i, to).start()
-        return 0
 
     for stage in range(STAGES):
         forward.hand_over(stage)
@@ -387,7 +385,8 @@
     for stage in range(STAGES):
         forward.arrive(stage)
         outputs(stage)
-    lax.fori_loop(0, blocks // NORM_BLOCKS, row_sums, 0)
+    for i in range(blocks // NORM_BLOCKS):
+        row_sums(i)
 
     def prefix_step(head, c):
         pre_bf[head, c] = (forward.carry[head] + pre[head, c]).astype(BF16)
@@ -444,20 +443,17 @@
     def k_step(head, c):
         tile(kp, c, head)[...] = flipped(w.at[head, c], tile(q, c, head))
 
-    grads(0)
-    grads(1)
-    backward.pair(0).start()
-    grads(2)
-    backward.pair(1).start()
-    grads(3)
-    backward.add_pair(0)
-    grads(4)
-    backward.add_pair(1)
+    for part in range(parts + 1):
+        grads(part)
+        if 0 < part <= STAGES:
+            backward.pair(part - 1).start()
+        if part > STAGES:
+            backward.add_pair(part - STAGES - 1)
     each(result_step)
     each(v_step)
-    each(dscore_step)
-    backward.add_chips(0)
-    backward.add_chips(1)
+    for stage in range(STAGES):
+        each(dscore_step, first=heads // STAGES * stage, last=heads // STAGES * (stage + 1))
+        backward.add_chips(stage)
     each(k_step)
     each(q_step)
     forward.drain()

time: 51.6 us -> 51.4 us (level)
  no operation moved by 1% of the time
where the time goes in v4:
time: 51.4 us; the launch traced here: 51.3 us
  Pallas kernels  50.5 us (98%)
  between operations  0.82 us (2%)
    pallas_call x1, Pallas kernels, on_device(): pl.pallas_call(main_kernel, out_shape=(flat, flat, flat32, flat32, flat,...  45.6 us
    pallas_call x1, Pallas kernels, on_device(): pl.pallas_call(last_kernel, out_shape=(like,) * 4, in_specs=[in_vmem] * 7...  4.81 us

profile of v4, /device:TPU:1, one launch (start us, length us, event | category | flops | bytes accessed | tf_op | source)
XLA Modules:
  0.0 51.3 jit_solution(7383930406567696395)
XLA Ops:
  0.6 45.6 %attention.1 = (bf16[1536,1024]{1,0:T(8,128)(2,1)S(1)}, bf16[1536,1024]{1,0:T(8,128)(2,1)S(1)}, f32[1536,1024]{1,0:T(8,128)S(1)}, f32[1536,1024]{1,0:T(8,128)S(1...) custom-call(bf16[1536,1024]{1,0:T(8,128)(2,1)} %q_hbm.1, ...), custom_call_target="tpu_custom_call" | custom-call | flops 4026531840 | bytes 12582912 | tf_op jit(solution)/shard_map/attention/pallas_call | solution.py:515
  46.3 4.8 %suffix_gradients.1 = (bf16[1536,1024]{1,0:T(8,128)(2,1)}, bf16[1536,1024]{1,0:T(8,128)(2,1)}, bf16[1536,1024]{1,0:T(8,128)(2,1)}, bf16[1536,1024]{1,0:T(8,128)(2,1)}) custom-call(bf16[1536,1024]{1,0:T(8,128)(2,1)S(1)} %get-tuple-element.11.res, bf16[1536,1024]{1,0:T(8,128)(2,1)S(1)} %get-tuple-element.12.qg, f32[1536,1024]{1,0:T(8,128)S(1)} %get-tuple-element.13.kp, ...), custom_call_target="tpu_custom_call" | custom-call | flops 805306368 | bytes 12582912 | tf_op jit(solution)/shard_map/suffix_gradients/pallas_call | solution.py:544
